TPU v7x, 32 devices: a whole 2x2x4 slice. The times are simulated.
32 devices in a mesh: batch: 8 (over y, x, core), mp: 4 (over z).
Axes of the slice: x: 2, y: 2, z: 4, core: 2. Of those that a mesh axis runs over, the one named last changes fastest.
Arguments:
- residual: bfloat16 [8, 64, 8192], P('batch', None, 'mp'), may hold values from -6 to 6
- query_states: bfloat16 [8, 64, 4096], P('batch', None, 'mp')
- key_states: bfloat16 [8, 64, 512], P('batch')
- value_states: bfloat16 [8, 64, 512], P('batch'), may hold values from -6 to 6
- prompt_perm: int32 [8], replicated, may hold values from 0 to 7, each once
- ablated_heads: int32 [8], replicated, may hold values from 0 to 31, as said below
- out_weight: bfloat16 [4096, 8192], P('batch', 'mp'), may hold values from -0.09375 to 0.09375
- rms_gain: float32 [8192], P('mp'), may hold values from 0.1 to 1.9
- gate_weight: bfloat16 [8192, 14336], P('mp', 'batch'), may hold values from -0.0625 to 0.0625
- up_weight: bfloat16 [8192, 14336], P('mp', 'batch'), may hold values from -0.0625 to 0.0625
- down_weight: bfloat16 [14336, 8192], P('batch', 'mp'), may hold values from -0.046875 to 0.046875
Outputs:
- attn_out: bfloat16 [8, 64, 8192], P('batch', None, 'mp')
- mlp_out: bfloat16 [8, 64, 8192], P('batch', None, 'mp')
Inputs may be any that keep to these rules, and one draw needn't show every extreme that they name: `prompt_perm`: each prompt index appears exactly once. `ablated_heads`: 8 different head indices in any order, one of them 32 - 1.
All inputs are finite; a program needn't handle non-finite values.
Results may differ from a plain program's by a relative error of at most 0.035.
Values may be sent and summed in bfloat16 or wider, within the bound.
A program may use at most 128 MiB of HBM per device.

v0:
```python
import math
import jax
import jax.numpy as jnp
from jax import lax
from jax.sharding import PartitionSpec as P

D = 8192
HEADS = 32
KV = 4
HD = 128
ABLATED = 8


def local_heads(query_states, key_states, value_states):
    prompts_here, length, columns = query_states.shape
    head_count = columns // HD
    first_head = lax.axis_index("mp") * head_count
    owners = (first_head + jnp.arange(head_count)) // (HEADS // KV)
    query_four = query_states.reshape(prompts_here, length, head_count, HD)
    key_four = jnp.take(key_states.reshape(prompts_here, length, KV, HD), owners, axis=2)
    value_four = jnp.take(value_states.reshape(prompts_here, length, KV, HD), owners, axis=2)
    scores = jnp.einsum(
        "pshd,pthd->phst", query_four, key_four, preferred_element_type=jnp.float32
    ) / math.sqrt(HD)
    positions = jnp.arange(length)
    causal = positions[:, None] >= positions[None, :]
    scores = jnp.where(causal, scores, -1e30)
    highest = jnp.max(scores, axis=-1, keepdims=True)
    weights = jnp.exp(scores - highest)
    probability = (weights / jnp.sum(weights, axis=-1, keepdims=True)).astype(jnp.bfloat16)
    mixed_heads = jnp.einsum(
        "phst,pthd->pshd", probability, value_four, preferred_element_type=jnp.float32
    )
    return mixed_heads.astype(jnp.bfloat16).reshape(prompts_here, length, head_count * HD)


def body(
    residual,
    query_states,
    key_states,
    value_states,
    prompt_perm,
    ablated_heads,
    out_weight,
    rms_gain,
    gate_weight,
    up_weight,
    down_weight,
):
    prompts_here, length, model_cols = residual.shape
    local_rows = prompts_here * length
    head_block = local_heads(query_states, key_states, value_states)
    all_heads = lax.all_gather(head_block, "mp", axis=2, tiled=True)
    batch_index = lax.axis_index("batch")
    sources = jnp.take(prompt_perm, batch_index * prompts_here + jnp.arange(prompts_here))
    stacked = all_heads.reshape(prompts_here, length, HEADS, HD)
    picked_cols = jnp.take(stacked, ablated_heads, axis=2).reshape(
        prompts_here, length * ABLATED * HD
    )
    block_rows = lax.all_gather(picked_cols, "batch", axis=0, tiled=True)
    selector = (sources[:, None] == jnp.arange(block_rows.shape[0])[None, :]).astype(jnp.bfloat16)
    picked = jnp.dot(selector, block_rows, preferred_element_type=jnp.float32)
    picked_four = picked.astype(jnp.bfloat16).reshape(prompts_here, length, ABLATED, HD)
    placing = (jnp.arange(HEADS)[:, None] == ablated_heads[None, :]).astype(jnp.bfloat16)
    placed = jnp.einsum(
        "psad,ga->psgd", picked_four, placing, preferred_element_type=jnp.float32
    ).astype(jnp.bfloat16)
    chosen = jnp.any(jnp.arange(HEADS)[:, None] == ablated_heads[None, :], axis=1)
    mixed_heads = jnp.where(chosen[None, None, :, None], placed, stacked).reshape(
        local_rows, HEADS * HD
    )
    attn_float = jnp.dot(
        mixed_heads,
        lax.all_gather(out_weight, "batch", axis=0, tiled=True),
        preferred_element_type=jnp.float32,
    )
    attn_out = attn_float.astype(jnp.bfloat16)
    hidden_state = residual.reshape(local_rows, model_cols).astype(jnp.float32) + attn_float
    squares = lax.psum(jnp.sum(hidden_state * hidden_state, axis=1), "mp")
    inverse = lax.rsqrt(squares / D + 1e-05)
    normed = (hidden_state * inverse[:, None] * rms_gain[None, :]).astype(jnp.bfloat16)
    block_rows = lax.all_gather(normed, "batch", axis=0, tiled=True)
    gate_part = jnp.dot(block_rows, gate_weight, preferred_element_type=jnp.float32)
    up_part = jnp.dot(block_rows, up_weight, preferred_element_type=jnp.float32)
    partial_value = jnp.concatenate([gate_part, up_part], axis=1)
    slice_width = gate_weight.shape[1]
    summed = lax.psum(partial_value.astype(jnp.bfloat16), "mp").astype(jnp.float32)
    hidden = (jax.nn.silu(summed[:, :slice_width]) * summed[:, slice_width:]).astype(jnp.bfloat16)
    block_rows = hidden
    mlp_float = lax.psum_scatter(
        jnp.dot(block_rows, down_weight, preferred_element_type=jnp.float32).astype(jnp.bfloat16),
        "batch",
        scatter_dimension=0,
        tiled=True,
    )
    return (
        attn_out.reshape(prompts_here, length, model_cols),
        mlp_float.reshape(prompts_here, length, model_cols),
    )


def solution(mesh):
    placed = (
        P("batch", None, "mp"),
        P("batch", None, "mp"),
        P("batch", None, None),
        P("batch", None, None),
        P(),
        P(),
        P("batch", "mp"),
        P("mp"),
        P("mp", "batch"),
        P("mp", "batch"),
        P("batch", "mp"),
    )
    return jax.shard_map(
        body,
        mesh=mesh,
        in_specs=placed,
        out_specs=(P("batch", None, "mp"), P("batch", None, "mp")),
        check_vma=False,
    )
```

profile of v0, /device:TPU:0, one launch (start us, length us, event | category | flops | bytes accessed | tf_op | source)
XLA Modules:
  0.0 413.6 jit_solution(484651136919230348)
XLA Ops:
  7.3 0.7 compare_select_fusion.1
  7.9 0.7 compare_and_fusion.1
  8.6 0.9 copy.37
  9.6 0.6 gather_fusion.2
  10.2 0.3 fusion.7
  10.5 0.9 bitcast_bitcast_fusion.1
  11.4 0.6 gather_fusion.1
  12.0 0.3 fusion.9
  12.3 17.4 %all_gather.12 = bf16[1,64,4096]{2,1,0:T(8,128)(2,1)S(1)} all-gather(bf16[1,64,1024]{2,1,0:T(8,128)(2,1)S(1)} %bitcast.109), channel_id=1, replica_groups=mesh['batch'=8,'mp'=4] {'mp'}, dimensions={2}, use_global_device_ids=true | all-gather | bytes 655360 | tf_op jit(solution)/shard_map/all_gather | solution.py:53
  29.6 0.1 copy.38
  29.7 0.2 copy.30
  30.0 0.6 gather_fusion
  30.6 0.1 copy.31
  30.7 0.8 reshape.200
  31.6 0.7 all-gather.5.cloned.1.call-update
  32.3 0.6 dynamic-slice.2
  33.6 27.7 %all-gather.9.cloned.1.call-done = bf16[8,1,65536]{2,1,0:T(2,128)(2,1)} async-done(((bf16[1,1,65536]{2,1,0:T(2,128)(2,1)}), bf16[8,1,65536]{2,1,0:T(2,128)(2,1)}) %all-gather.9.cloned.1.call-update) | async-done | bytes 1048592 | tf_op jit(solution)/shard_map/all_gather | solution.py:60
  61.3 2.9 fusion.11
  64.2 0.4 fusion.10
  64.6 88.5 %all-gather.5.cloned.1.call-done = bf16[4096,2048]{1,0:T(8,128)(2,1)} async-done(((bf16[512,2048]{1,0:T(8,128)(2,1)}), bf16[4096,2048]{1,0:T(8,128)(2,1)}) %all-gather.5.cloned.1.call-update) | async-done | bytes 16777232 | tf_op jit(solution)/shard_map/all_gather | solution.py:74
  153.1 8.9 %multiply_reduce_fusion = (f32[64]{0:T(128)S(1)}, f32[64,2048]{1,0:T(8,128)S(1)}) fusion(bf16[1,64,2048]{2,1,0:T(8,128)(2,1)S(1)} %copy-done.2, bf16[4096,2048]{1,0:T(8,128)(2,1)} %all-gather.5.cloned.1.call-done, bf16[8,8,32,128]{3,2,1,0:T(8,128)(2,1)S(1)} %bitcast.106), kind=kOutput, calls=%fused_computation.29 | convolution fusion | flops 1074266112 | bytes 18088192 | tf_op jit(solution)/shard_map/dot_general | solution.py:72
  162.0 11.7 %psum.14 = f32[64]{0:T(128)S(1)} all-reduce(f32[64]{0:T(128)S(1)} %get-tuple-element.16), channel_id=1, replica_groups=mesh['batch'=8,'mp'=4] {'mp'}, use_global_device_ids=true, to_apply=%region_4.6 | all-reduce | flops 64 | bytes 512 | tf_op jit(solution)/shard_map/psum | solution.py:79
  173.7 0.8 multiply_convert_fusion
  174.6 0.2 all-reduce.2.cloned.1.call-start
  174.8 25.1 %all-gather.7.cloned.1.call-done = bf16[512,2048]{1,0:T(8,128)(2,1)} async-done(((bf16[64,2048]{1,0:T(8,128)(2,1)}), bf16[512,2048]{1,0:T(8,128)(2,1)}) %all-gather.7.cloned.1.call-update) | async-done | bytes 2097168 | tf_op jit(solution)/shard_map/all_gather | solution.py:82
  199.9 7.8 %convolution_convert_fusion.1 = bf16[512,1792]{1,0:T(8,128)(2,1)S(1)} fusion(bf16[512,2048]{1,0:T(8,128)(2,1)} %all-gather.7.cloned.1.call-done, bf16[2048,1792]{1,0:T(8,128)(2,1)} %param.22), kind=kOutput, calls=%fused_computation.8 | convolution fusion | flops 3759013888 | bytes 11272192 | tf_op jit(solution)/shard_map/dot_general | solution.py:84
  207.7 7.0 %convolution_convert_fusion.2 = bf16[512,1792]{1,0:T(8,128)(2,1)S(1)} fusion(bf16[512,2048]{1,0:T(8,128)(2,1)S(1)} %copy-done.5, bf16[2048,1792]{1,0:T(8,128)(2,1)} %param.21), kind=kOutput, calls=%fused_computation.9 | convolution fusion | flops 3759013888 | bytes 11272192 | tf_op jit(solution)/shard_map/dot_general | solution.py:83
  214.7 2.1 pad_maximum_fusion
  216.9 138.2 %all-reduce.2.cloned.1.call-done = bf16[512,3584]{1,0:T(8,128)(2,1)} async-done(((bf16[512,3584]{1,0:T(8,128)(2,1)}), bf16[512,3584]{1,0:T(8,128)(2,1)}) %all-reduce.2.cloned.1.call-update) | async-done | bytes 3670032 | tf_op jit(solution)/shard_map/psum | solution.py:87
  355.1 3.0 convert_element_type.62
  358.1 8.5 %convolution_convert_fusion = bf16[512,2048]{1,0:T(8,128)(2,1)} fusion(bf16[1792,2048]{1,0:T(8,128)(2,1)} %param.23, f32[512,3584]{1,0:T(8,128)S(1)} %convert_element_type.62), kind=kOutput, calls=%fused_computation.7 | convolution fusion | flops 3764649984 | bytes 16777216 | tf_op jit(solution)/shard_map/dot_general | solution.py:91
  366.7 40.4 %reduce-scatter.2.cloned.1.call-done = bf16[64,2048]{1,0:T(8,128)(2,1)} async-done(((bf16[512,2048]{1,0:T(8,128)(2,1)}), bf16[64,2048]{1,0:T(8,128)(2,1)}) %reduce-scatter.2.cloned.1.call-update) | async-done | bytes 262160 | tf_op jit(solution)/shard_map/reduce_scatter | solution.py:90
  (33 shorter events, 0.6 us)
Async XLA Ops:
  7.2 1.5 copy-start
  7.2 54.1 %all-gather.9.cloned.1.call-start = ((), (), s32[]{:S(2)}) async-start(), calls=%async_computation.5 | async-start | bytes 2359296 | tf_op jit(solution)/shard_map/all_gather | solution.py:60
  11.9 20.4 %copy-start.6 = (s32[8]{0:T(128)S(1)}, s32[8]{0:T(128)}, u32[]{:S(2)}) copy-start(s32[8]{0:T(128)} %param.17) | copy-start | bytes 100
  12.0 21.6 %copy-start.4 = (s32[8]{0:T(128)S(1)}, s32[8]{0:T(128)}, u32[]{:S(2)}) copy-start(s32[8]{0:T(128)} %param.18) | copy-start | bytes 100
  29.7 123.4 %copy-start.2 = (bf16[1,64,2048]{2,1,0:T(8,128)(2,1)S(1)}, bf16[1,64,2048]{2,1,0:T(8,128)(2,1)}, u32[]{:S(2)}) copy-start(bf16[1,64,2048]{2,1,0:T(8,128)(2,1)} %param.13) | copy-start | bytes 786436
  31.5 121.6 %all-gather.5.cloned.1.call-start = ((), (), s32[]{:S(2)}) async-start(), calls=%async_computation.1 | async-start | bytes 18874368 | tf_op jit(solution)/shard_map/all_gather | solution.py:74
  32.3 167.6 %all-gather.7.cloned.1.call-start = ((), (), s32[]{:S(2)}) async-start(), calls=%async_computation.2 | async-start | bytes 2359296 | tf_op jit(solution)/shard_map/all_gather | solution.py:82
  153.1 20.6 %copy-start.3 = (f32[2048]{0:T(1024)S(1)}, f32[2048]{0:T(1024)}, u32[]{:S(2)}) copy-start(f32[2048]{0:T(1024)} %param.20) | copy-start | bytes 24580
  174.6 180.5 %all-reduce.2.cloned.1.call-start = ((), (), s32[]{:S(2)}) async-start(), calls=%async_computation.3 | async-start | bytes 7340032 | tf_op jit(solution)/shard_map/psum | solution.py:87
  199.9 7.8 %copy-start.5 = (bf16[512,2048]{1,0:T(8,128)(2,1)S(1)}, bf16[512,2048]{1,0:T(8,128)(2,1)}, u32[]{:S(2)}) copy-start(bf16[512,2048]{1,0:T(8,128)(2,1)} %all-gather.7.cloned.1.call-done) | copy-start | bytes 6291460
  216.9 190.2 %reduce-scatter.2.cloned.1.call-start = ((), (), s32[]{:S(2)}) async-start(), calls=%async_computation.4 | async-start | bytes 2359296 | tf_op jit(solution)/shard_map/reduce_scatter | solution.py:90
  358.1 49.0 %copy-start.1 = (bf16[1,64,512]{2,1,0:T(8,128)(2,1)S(1)}, bf16[1,64,512]{2,1,0:T(8,128)(2,1)}, u32[]{:S(2)}) copy-start(bf16[1,64,512]{2,1,0:T(8,128)(2,1)} %param.15) | copy-start | bytes 196612
Sparse Core Ops, SparseCore 0:
  31.6 29.6 all-gather.8
  63.2 89.8 all-gather.4
  174.7 25.1 all-gather.6
  217.0 138.0 all-reduce.1
  366.8 40.2 reduce-scatter.1
where the time goes:
time: 414 us
  waiting for transfers between devices  321 us (78%)
  matrix products  36.1 us (9%)
  blocking collectives  29.1 us (7%)
  between operations  14.6 us (4%)
  other arithmetic  7.56 us (2%)
  local copies, waits for them, and re-layouts  5.31 us (1%)
    psum x1, waiting for transfers between devices, body(): lax.psum(partial_value.astype(jnp.bfloat16), 'mp').astype(jnp.float32)  138 us
    all_gather x1, waiting for transfers between devices, body(): lax.all_gather(out_weight, 'batch', axis=0, tiled=True)  88.5 us
    reduce_scatter x1, waiting for transfers between devices, body(): lax.psum_scatter(jnp.dot(block_rows, down_weight, preferred_element_type=...  40.4 us
    all_gather x1, waiting for transfers between devices, body(): block_rows = lax.all_gather(picked_cols, 'batch', axis=0, tiled=True)  27.7 us
    all_gather x1, waiting for transfers between devices, body(): block_rows = lax.all_gather(normed, 'batch', axis=0, tiled=True)  25.1 us
    all_gather x1, blocking collectives, body(): all_heads = lax.all_gather(head_block, 'mp', axis=2, tiled=True)  17.4 us
    psum x1, blocking collectives, body(): squares = lax.psum(jnp.sum(hidden_state * hidden_state, axis=1), 'mp')  11.7 us
    dot_general x1, matrix products, body(): jnp.dot(mixed_heads, lax.all_gather(out_weight, 'batch', axis=0, tiled=Tr...  8.92 us
  transfers between devices with their start and end apart: 5, of which 5 were waited for; matrix products, arithmetic and copies ran while one was open for 1% of the time, Pallas kernels for 0%

commit v1 on v0

--- a/solution.py
+++ b/solution.py
@@ -47,6 +47,21 @@
     up_weight,
     down_weight,
 ):
+
+    def racks_point(a0):
+        device_axis = "batch"
+        n_lanes = jax.lax.axis_size(device_axis)
+        frames = [a0]
+        for t in [*range(n_lanes - 1)]:
+            frames.append(
+                jax.lax.ppermute(
+                    frames[-1], device_axis, [(kk, (kk + 1) % n_lanes) for kk in range(n_lanes)]
+                )
+            )
+        return jnp.roll(
+            jnp.concatenate(frames[::-1], 0), (jax.lax.axis_index(device_axis) + 1) * a0.shape[0], 0
+        )
+
     prompts_here, length, model_cols = residual.shape
     local_rows = prompts_here * length
     head_block = local_heads(query_states, key_states, value_states)
@@ -57,7 +72,7 @@
     picked_cols = jnp.take(stacked, ablated_heads, axis=2).reshape(
         prompts_here, length * ABLATED * HD
     )
-    block_rows = lax.all_gather(picked_cols, "batch", axis=0, tiled=True)
+    block_rows = racks_point(picked_cols)
     selector = (sources[:, None] == jnp.arange(block_rows.shape[0])[None, :]).astype(jnp.bfloat16)
     picked = jnp.dot(selector, block_rows, preferred_element_type=jnp.float32)
     picked_four = picked.astype(jnp.bfloat16).reshape(prompts_here, length, ABLATED, HD)

time: 414 us -> 385 us (0.930)
  waiting for transfers between devices: 321 us -> 282 us
  local copies, waits for them, and re-layouts: 5.31 us -> 18.1 us
    all_gather x1, waiting for transfers between devices: 88.5 us -> 0.02 us  [body(): lax.all_gather(out_weight, 'batch', axis=0, tiled=True)]
    ppermute x0 -> x7, waiting for transfers between devices: none -> 78.7 us  [racks_point(): jax.lax.ppermute(frames[-1], device_axis, [(kk, (kk + 1) % n_lanes) for k...]
    all_gather x1 -> x0, waiting for transfers between devices: 27.7 us -> none  [body(): block_rows = lax.all_gather(picked_cols, 'batch', axis=0, tiled=True)]
    concatenate x0 -> x1, local copies, waits for them, and re-layouts: none -> 10.6 us  [racks_point(): jnp.roll(jnp.concatenate(frames[::-1], 0), (jax.lax.axis_index(device_axi...]
  transfers between devices with their start and end apart: 5 -> 11, of which waited for: 5 -> 10; matrix products, arithmetic and copies ran while one was open for 1% -> 4% of each run, Pallas kernels for 0% -> 0%
where the time goes in v1:
time: 385 us; the launch traced here: 384 us
  waiting for transfers between devices  282 us (73%)
  matrix products  33.6 us (9%)
  blocking collectives  29 us (8%)
  local copies, waits for them, and re-layouts  18.1 us (5%)
  between operations  14.7 us (4%)
  other arithmetic  6.24 us (2%)
    psum x1, waiting for transfers between devices, body(): lax.psum(partial_value.astype(jnp.bfloat16), 'mp').astype(jnp.float32)  138 us
    ppermute x7, waiting for transfers between devices, racks_point(): jax.lax.ppermute(frames[-1], device_axis, [(kk, (kk + 1) % n_lanes) for k...  78.7 us
    reduce_scatter x1, waiting for transfers between devices, body(): lax.psum_scatter(jnp.dot(block_rows, down_weight, preferred_element_type=...  40.4 us
    all_gather x1, waiting for transfers between devices, body(): block_rows = lax.all_gather(normed, 'batch', axis=0, tiled=True)  24.1 us
    all_gather x1, blocking collectives, body(): all_heads = lax.all_gather(head_block, 'mp', axis=2, tiled=True)  17.4 us
    psum x1, blocking collectives, body(): squares = lax.psum(jnp.sum(hidden_state * hidden_state, axis=1), 'mp')  11.7 us
    concatenate x1, local copies, waits for them, and re-layouts, racks_point(): jnp.roll(jnp.concatenate(frames[::-1], 0), (jax.lax.axis_index(device_axi...  10.6 us
    dot_general x1, matrix products, body(): jnp.dot(mixed_heads, lax.all_gather(out_weight, 'batch', axis=0, tiled=Tr...  8.91 us
  transfers between devices with their start and end apart: 11, of which 10 were waited for; matrix products, arithmetic and copies ran while one was open for 4% of the time, Pallas kernels for 0%

profile of v1, /device:TPU:0, one launch (start us, length us, event | category | flops | bytes accessed | tf_op | source)
XLA Modules:
  0.0 384.3 jit_solution(17536130863115360362)
XLA Ops:
  7.2 0.7 all-gather.3.cloned.1.call-update
  8.0 0.9 copy.29
  9.0 0.6 gather_fusion.2
  9.6 0.9 bitcast_bitcast_fusion.1
  10.4 0.6 gather_fusion.1
  11.7 17.4 %all_gather.9 = bf16[1,64,4096]{2,1,0:T(8,128)(2,1)S(1)} all-gather(bf16[1,64,1024]{2,1,0:T(8,128)(2,1)S(1)} %bitcast.106), channel_id=1, replica_groups=mesh['batch'=8,'mp'=4] {'mp'}, dimensions={2}, use_global_device_ids=true | all-gather | bytes 655360 | tf_op jit(solution)/shard_map/all_gather | solution.py:68
  29.4 0.6 gather_fusion
  30.3 12.3 %collective-permute-done = bf16[1,65536]{1,0:T(2,128)(2,1)S(1)} collective-permute-done((bf16[1,65536]{1,0:T(2,128)(2,1)S(1)}, bf16[1,65536]{1,0:T(2,128)(2,1)S(1)}, u32[]{:S(2)}, u32[]{:S(2)}) %collective-permute-start) | collective-permute-done | bytes 131104 | tf_op jit(solution)/shard_map/ppermute | solution.py:57
  42.6 10.8 %collective-permute-done.1 = bf16[1,65536]{1,0:T(2,128)(2,1)S(1)} collective-permute-done((bf16[1,65536]{1,0:T(2,128)(2,1)S(1)}, bf16[1,65536]{1,0:T(2,128)(2,1)S(1)}, u32[]{:S(2)}, u32[]{:S(2)}) %collective-permute-start.1) | collective-permute-done | bytes 131104 | tf_op jit(solution)/shard_map/ppermute | solution.py:57
  53.4 0.7 copy-done.3
  54.1 7.8 %collective-permute-done.2 = bf16[1,65536]{1,0:T(2,128)(2,1)S(1)} collective-permute-done((bf16[1,65536]{1,0:T(2,128)(2,1)S(1)}, bf16[1,65536]{1,0:T(2,128)(2,1)S(1)}, u32[]{:S(2)}, u32[]{:S(2)}) %collective-permute-start.2) | collective-permute-done | bytes 131104 | tf_op jit(solution)/shard_map/ppermute | solution.py:57
  61.9 0.7 copy-done.4
  62.6 12.3 %collective-permute-done.3 = bf16[1,65536]{1,0:T(2,128)(2,1)S(1)} collective-permute-done((bf16[1,65536]{1,0:T(2,128)(2,1)S(1)}, bf16[1,65536]{1,0:T(2,128)(2,1)S(1)}, u32[]{:S(2)}, u32[]{:S(2)}) %collective-permute-start.3) | collective-permute-done | bytes 131104 | tf_op jit(solution)/shard_map/ppermute | solution.py:57
  74.8 0.7 copy-done.5
  75.6 12.3 %collective-permute-done.4 = bf16[1,65536]{1,0:T(2,128)(2,1)S(1)} collective-permute-done((bf16[1,65536]{1,0:T(2,128)(2,1)S(1)}, bf16[1,65536]{1,0:T(2,128)(2,1)S(1)}, u32[]{:S(2)}, u32[]{:S(2)}) %collective-permute-start.4) | collective-permute-done | bytes 131104 | tf_op jit(solution)/shard_map/ppermute | solution.py:57
  87.8 0.7 copy-done.6
  88.5 12.3 %collective-permute-done.5 = bf16[1,65536]{1,0:T(2,128)(2,1)S(1)} collective-permute-done((bf16[1,65536]{1,0:T(2,128)(2,1)S(1)}, bf16[1,65536]{1,0:T(2,128)(2,1)S(1)}, u32[]{:S(2)}, u32[]{:S(2)}) %collective-permute-start.5) | collective-permute-done | bytes 131104 | tf_op jit(solution)/shard_map/ppermute | solution.py:57
  100.8 0.7 dynamic-slice.2
  102.2 11.0 %collective-permute-done.6 = bf16[1,65536]{1,0:T(2,128)(2,1)} collective-permute-done((bf16[1,65536]{1,0:T(2,128)(2,1)S(1)}, bf16[1,65536]{1,0:T(2,128)(2,1)}, u32[]{:S(2)}, u32[]{:S(2)}) %collective-permute-start.6) | collective-permute-done | bytes 131104 | tf_op jit(solution)/shard_map/ppermute | solution.py:57
  113.2 10.6 %concatenate.10 = bf16[16,65536]{1,0:T(8,128)(2,1)S(1)} concatenate(bf16[1,65536]{1,0:T(2,128)(2,1)} %collective-permute-done.6, bf16[1,65536]{1,0:T(2,128)(2,1)} %copy-done.7, bf16[1,65536]{1,0:T(2,128)(2,1)} %copy-done.6, bf16[1,65536]{1,0:T(2,128)(2,1)} %copy-done.5, bf16[1,65536]{1,0:T(2,128)(2,1)} %copy-done.4, bf16[1,65536]{1,0:T(2,128)(2,1)} %copy-done.3, ...), dimensions={0} | concatenate | bytes 4194304 | tf_op jit(solution)/shard_map/jit(_roll_dynamic)/concatenate | solution.py:61
  123.8 0.4 fusion.11
  124.7 8.9 %multiply_reduce_fusion = (f32[64]{0:T(128)S(1)}, f32[64,2048]{1,0:T(8,128)S(1)}) fusion(bf16[1,64,2048]{2,1,0:T(8,128)(2,1)S(1)} %copy-done.2, bf16[4096,2048]{1,0:T(8,128)(2,1)} %all-gather.3.cloned.1.call-done, bf16[8,8,32,128]{3,2,1,0:T(8,128)(2,1)S(1)} %bitcast.103), kind=kOutput, calls=%fused_computation.28 | convolution fusion | flops 1074266112 | bytes 18088192 | tf_op jit(solution)/shard_map/dot_general | solution.py:87
  133.6 11.7 %psum.14 = f32[64]{0:T(128)S(1)} all-reduce(f32[64]{0:T(128)S(1)} %get-tuple-element.16), channel_id=1, replica_groups=mesh['batch'=8,'mp'=4] {'mp'}, use_global_device_ids=true, to_apply=%region_4.6 | all-reduce | flops 64 | bytes 512 | tf_op jit(solution)/shard_map/psum | solution.py:94
  145.3 0.8 multiply_convert_fusion
  146.4 24.1 %all-gather.5.cloned.1.call-done = bf16[512,2048]{1,0:T(8,128)(2,1)} async-done(((bf16[64,2048]{1,0:T(8,128)(2,1)}), bf16[512,2048]{1,0:T(8,128)(2,1)}) %all-gather.5.cloned.1.call-update) | async-done | bytes 2097168 | tf_op jit(solution)/shard_map/all_gather | solution.py:97
  170.6 7.8 %convolution_convert_fusion.1 = bf16[512,1792]{1,0:T(8,128)(2,1)S(1)} fusion(bf16[512,2048]{1,0:T(8,128)(2,1)} %all-gather.5.cloned.1.call-done, bf16[2048,1792]{1,0:T(8,128)(2,1)} %param.22), kind=kOutput, calls=%fused_computation.8 | convolution fusion | flops 3759013888 | bytes 11272192 | tf_op jit(solution)/shard_map/dot_general | solution.py:99
  178.4 7.0 %convolution_convert_fusion.2 = bf16[512,1792]{1,0:T(8,128)(2,1)S(1)} fusion(bf16[512,2048]{1,0:T(8,128)(2,1)S(1)} %copy-done.10, bf16[2048,1792]{1,0:T(8,128)(2,1)} %param.21), kind=kOutput, calls=%fused_computation.9 | convolution fusion | flops 3759013888 | bytes 11272192 | tf_op jit(solution)/shard_map/dot_general | solution.py:98
  185.4 2.1 pad_maximum_fusion
  187.6 138.2 %all-reduce.2.cloned.1.call-done = bf16[512,3584]{1,0:T(8,128)(2,1)} async-done(((bf16[512,3584]{1,0:T(8,128)(2,1)}), bf16[512,3584]{1,0:T(8,128)(2,1)}) %all-reduce.2.cloned.1.call-update) | async-done | bytes 3670032 | tf_op jit(solution)/shard_map/psum | solution.py:102
  325.8 3.0 convert_element_type.62
  328.8 8.5 %convolution_convert_fusion = bf16[512,2048]{1,0:T(8,128)(2,1)} fusion(bf16[1792,2048]{1,0:T(8,128)(2,1)} %param.23, f32[512,3584]{1,0:T(8,128)S(1)} %convert_element_type.62), kind=kOutput, calls=%fused_computation.7 | convolution fusion | flops 3764649984 | bytes 16777216 | tf_op jit(solution)/shard_map/dot_general | solution.py:106
  337.3 40.4 %reduce-scatter.2.cloned.1.call-done = bf16[64,2048]{1,0:T(8,128)(2,1)} async-done(((bf16[512,2048]{1,0:T(8,128)(2,1)}), bf16[64,2048]{1,0:T(8,128)(2,1)}) %reduce-scatter.2.cloned.1.call-update) | async-done | bytes 262160 | tf_op jit(solution)/shard_map/reduce_scatter | solution.py:105
  (55 shorter events, 2.2 us)
Async XLA Ops:
  7.2 1.8 copy-start
  7.2 117.5 %all-gather.3.cloned.1.call-start = ((), (), s32[]{:S(2)}) async-start(), calls=%async_computation.1 | async-start | bytes 18874368 | tf_op jit(solution)/shard_map/all_gather | solution.py:89
  7.9 21.4 %copy-start.9 = (s32[8]{0:T(128)S(1)}, s32[8]{0:T(128)}, u32[]{:S(2)}) copy-start(s32[8]{0:T(128)} %param.18) | copy-start | bytes 100
  7.9 162.7 %all-gather.5.cloned.1.call-start = ((), (), s32[]{:S(2)}) async-start(), calls=%async_computation.2 | async-start | bytes 2359296 | tf_op jit(solution)/shard_map/all_gather | solution.py:97
  8.9 91.9 %copy-start.11 = (s32[8]{0:T(128)S(1)}, s32[8]{0:T(128)}, u32[]{:S(2)}) copy-start(s32[8]{0:T(128)} %param.17) | copy-start | bytes 100
  30.2 12.3 %collective-permute-start = (bf16[1,65536]{1,0:T(2,128)(2,1)S(1)}, bf16[1,65536]{1,0:T(2,128)(2,1)S(1)}, u32[]{:S(2)}, u32[]{:S(2)}) collective-permute-start(bf16[1,65536]{1,0:T(2,128)(2,1)S(1)} %reshape.199), channel_id=1, source_target_pairs={{0,4},{4,8},{8,12},{12,16},{16,20},{20,24},{24,28},{28,0},{1,5},{5... | collective-permute-start | bytes 393224 | tf_op jit(solution)/shard_map/ppermute | solution.py:57
  42.6 10.8 %collective-permute-start.1 = (bf16[1,65536]{1,0:T(2,128)(2,1)S(1)}, bf16[1,65536]{1,0:T(2,128)(2,1)S(1)}, u32[]{:S(2)}, u32[]{:S(2)}) collective-permute-start(bf16[1,65536]{1,0:T(2,128)(2,1)S(1)} %collective-permute-done), channel_id=1, source_target_pairs={{0,4},{4,8},{8,12},{12,16},{16,20},{20,24},{24,28},{28,0},{1,5},{5... | collective-permute-start | bytes 393224 | tf_op jit(solution)/shard_map/ppermute | solution.py:57
  53.4 0.7 copy-start.3
  54.1 7.8 %collective-permute-start.2 = (bf16[1,65536]{1,0:T(2,128)(2,1)S(1)}, bf16[1,65536]{1,0:T(2,128)(2,1)S(1)}, u32[]{:S(2)}, u32[]{:S(2)}) collective-permute-start(bf16[1,65536]{1,0:T(2,128)(2,1)S(1)} %collective-permute-done.1), channel_id=1, source_target_pairs={{0,4},{4,8},{8,12},{12,16},{16,20},{20,24},{24,28},{28,0},{1,5},{5... | collective-permute-start | bytes 393224 | tf_op jit(solution)/shard_map/ppermute | solution.py:57
  61.9 0.7 copy-start.4
  62.6 12.3 %collective-permute-start.3 = (bf16[1,65536]{1,0:T(2,128)(2,1)S(1)}, bf16[1,65536]{1,0:T(2,128)(2,1)S(1)}, u32[]{:S(2)}, u32[]{:S(2)}) collective-permute-start(bf16[1,65536]{1,0:T(2,128)(2,1)S(1)} %collective-permute-done.2), channel_id=1, source_target_pairs={{0,4},{4,8},{8,12},{12,16},{16,20},{20,24},{24,28},{28,0},{1,5},{5... | collective-permute-start | bytes 393224 | tf_op jit(solution)/shard_map/ppermute | solution.py:57
  74.8 0.7 copy-start.5
  75.6 12.3 %collective-permute-start.4 = (bf16[1,65536]{1,0:T(2,128)(2,1)S(1)}, bf16[1,65536]{1,0:T(2,128)(2,1)S(1)}, u32[]{:S(2)}, u32[]{:S(2)}) collective-permute-start(bf16[1,65536]{1,0:T(2,128)(2,1)S(1)} %collective-permute-done.3), channel_id=1, source_target_pairs={{0,4},{4,8},{8,12},{12,16},{16,20},{20,24},{24,28},{28,0},{1,5},{5... | collective-permute-start | bytes 393224 | tf_op jit(solution)/shard_map/ppermute | solution.py:57
  87.8 0.7 copy-start.6
  88.5 12.3 %collective-permute-start.5 = (bf16[1,65536]{1,0:T(2,128)(2,1)S(1)}, bf16[1,65536]{1,0:T(2,128)(2,1)S(1)}, u32[]{:S(2)}, u32[]{:S(2)}) collective-permute-start(bf16[1,65536]{1,0:T(2,128)(2,1)S(1)} %collective-permute-done.4), channel_id=1, source_target_pairs={{0,4},{4,8},{8,12},{12,16},{16,20},{20,24},{24,28},{28,0},{1,5},{5... | collective-permute-start | bytes 393224 | tf_op jit(solution)/shard_map/ppermute | solution.py:57
  100.8 1.4 copy-start.7
  100.8 12.4 %collective-permute-start.6 = (bf16[1,65536]{1,0:T(2,128)(2,1)S(1)}, bf16[1,65536]{1,0:T(2,128)(2,1)}, u32[]{:S(2)}, u32[]{:S(2)}) collective-permute-start(bf16[1,65536]{1,0:T(2,128)(2,1)S(1)} %collective-permute-done.5), channel_id=1, source_target_pairs={{0,4},{4,8},{8,12},{12,16},{16,20},{20,24},{24,28},{28,0},{1,5},{5... | collective-permute-start | bytes 393224 | tf_op jit(solution)/shard_map/ppermute | solution.py:57
  102.2 22.5 %copy-start.2 = (bf16[1,64,2048]{2,1,0:T(8,128)(2,1)S(1)}, bf16[1,64,2048]{2,1,0:T(8,128)(2,1)}, u32[]{:S(2)}) copy-start(bf16[1,64,2048]{2,1,0:T(8,128)(2,1)} %param.13) | copy-start | bytes 786436
  124.7 20.6 %copy-start.8 = (f32[2048]{0:T(1024)S(1)}, f32[2048]{0:T(1024)}, u32[]{:S(2)}) copy-start(f32[2048]{0:T(1024)} %param.20) | copy-start | bytes 24580
  146.2 179.6 %all-reduce.2.cloned.1.call-start = ((), (), s32[]{:S(2)}) async-start(), calls=%async_computation.3 | async-start | bytes 7340032 | tf_op jit(solution)/shard_map/psum | solution.py:102
  170.6 7.8 %copy-start.10 = (bf16[512,2048]{1,0:T(8,128)(2,1)S(1)}, bf16[512,2048]{1,0:T(8,128)(2,1)}, u32[]{:S(2)}) copy-start(bf16[512,2048]{1,0:T(8,128)(2,1)} %all-gather.5.cloned.1.call-done) | copy-start | bytes 6291460
  187.6 190.2 %reduce-scatter.2.cloned.1.call-start = ((), (), s32[]{:S(2)}) async-start(), calls=%async_computation.4 | async-start | bytes 2359296 | tf_op jit(solution)/shard_map/reduce_scatter | solution.py:105
  328.8 49.0 %copy-start.1 = (bf16[1,64,512]{2,1,0:T(8,128)(2,1)S(1)}, bf16[1,64,512]{2,1,0:T(8,128)(2,1)}, u32[]{:S(2)}) copy-start(bf16[1,64,512]{2,1,0:T(8,128)(2,1)} %param.15) | copy-start | bytes 196612
Sparse Core Ops, SparseCore 0:
  9.9 109.5 all-gather.2
  146.3 24.2 all-gather.4
  187.7 138.0 all-reduce.1
  337.5 40.2 reduce-scatter.1
